TPU v7x, 32 devices: a whole 2x2x4 slice. The times are simulated.
32 devices in a mesh: grp: 2 (over x), req: 8 (over z, y), head: 2 (over core).
Axes of the slice: x: 2, y: 2, z: 4, core: 2. Of those that a mesh axis runs over, the one named last changes fastest.
Arguments:
- x_rows: bfloat16 [22528, 8192], P(('grp', 'req'), 'head'), parts along dimension 0, may hold values from -6 to 6
- b_rows: bfloat16 [22528, 1024], P(('grp', 'req'), 'head'), parts along dimension 0, may hold values from -0.59765625 to 0.59765625
- c_rows: bfloat16 [22528, 1024], P(('grp', 'req'), 'head'), parts along dimension 0, may hold values from -6 to 6
- time_step: bfloat16 [128, 22528], P('head', ('grp', 'req')), parts along dimension 1, may hold values from 0 to 4
- decay_log: float32 [128], P('head'), may hold values from -3 to 1
- skip_gain: float32 [128], P('head'), may hold values from 0.1 to 1.9
- prompt_lengths: int32 [16], P('grp'), parts along dimension 0, may hold values from 1 to 1408, as said below
- block_lists: int32 [16, 6], P('grp'), parts along dimension 0, may hold values from 0 to 82, as said below
- decode_slot: int32 [16], P('grp'), parts along dimension 0, may hold values from 0 to 11, as said below
- staying: int32 [16], P('grp'), parts along dimension 0, may hold values from 0 to 1, as said below
Outputs:
- layer_out: bfloat16 [12288, 8192], P(('grp', 'req'), 'head'), parts along dimension 0
- kept_states: float32 [16, 128, 64, 128], P(('grp', 'req'), 'head'), parts along dimension 0
- decode_states: float32 [16, 2, 8, 12, 64, 128], P(('grp', 'req'), 'head'), parts along dimension 0
There are 2 independent parts, one for each index of `grp`. A program takes and returns all parts, laid end to end along the dimension named above; an argument that names none is the same for every part. Nothing has to cross between parts.
Inputs may be any that keep to these rules, and one draw needn't show every extreme that they name: `prompt_lengths`: request r fills nb[r] = ceil(length / 128) slots, nb[r] = 6 + e[r] - e[r-1] with whole numbers 0 <= e[r] <= 5, e[-1] = e[7] = 0, e[6] = 5; some request fills all 11 slots. `block_lists`: row p lists the last e[p-1] filled slots of request p-1, then the first 6 - e[p-1] slots of request p, each in order (e as for prompt_lengths); every filled slot is listed once. `decode_slot`: distinct slots; slot 0 and slot 11 are used. `staying`: both values occur.
All inputs are finite; a program needn't handle non-finite values.
Results may differ from a plain program's by a relative error of at most 0.0043.
Values may be sent and summed in bfloat16 or wider, within the bound.
No kernel may reach another device: no remote copies, remote signals or barrier semaphores. Data moves between devices by JAX's collectives and lax.ppermute only.
A program may use at most 128 MiB of HBM per device.

v0:
```python
import math

import jax
import jax.numpy as jnp
from jax import lax
from jax.experimental import pallas as pl
from jax.experimental.pallas import tpu as pltpu
from jax.sharding import PartitionSpec as P

N = 128
TILE = 128
W = 6
TAIL = W - 1
DCAP = 12
DEC_REQ = 8
SLOTS = 11
VMEM = 58 * 1024 * 1024
CEILING = 64.0
LOG2E = math.log2(math.e)
F32 = jnp.float32
BF16 = jnp.bfloat16


def shifted(block, axis, distance):
    devices = range(lax.axis_size(axis))
    route = [(i - distance, i) for i in devices if i - distance in devices]
    return lax.ppermute(block, axis, route)


def prepare(prompt_lengths, decode_slot, staying, decay_log, skip_gain):
    req_count = prompt_lengths.shape[0]
    head_count = decay_log.shape[0]

    def kernel(lengths, slots, stays, decay_ref, skip_ref, meta, source, gains):
        device = lax.axis_index("req")
        blocks = lambda r: (lengths[r] + TILE - 1) // TILE
        before = jnp.int32(0)
        for r in range(req_count):
            before += jnp.where(r < device, blocks(r) - W, 0)
        meta[0] = lengths[device]
        meta[1] = blocks(device)
        meta[2] = before
        meta[3] = stays[device]
        first = (device // DEC_REQ) * DCAP
        for c in range(DCAP):
            found = jnp.int32(-1)
            for r in range(req_count):
                found = jnp.where((slots[r] == first + c) & (stays[r] == 0), r, found)
            source[c] = found
        spread = lambda row: jnp.broadcast_to(row, (TILE, head_count)).T
        gains[0] = spread(-LOG2E * jnp.exp(decay_ref[...]))
        gains[1] = spread(skip_ref[...])

    smem = pl.BlockSpec(memory_space=pltpu.SMEM)
    vmem = pl.BlockSpec(memory_space=pltpu.VMEM)
    return pl.pallas_call(
        kernel,
        in_specs=[smem, smem, smem, vmem, vmem],
        out_specs=[smem, smem, vmem],
        out_shape=[
            jax.ShapeDtypeStruct((4,), jnp.int32),
            jax.ShapeDtypeStruct((DCAP,), jnp.int32),
            jax.ShapeDtypeStruct((2, head_count, TILE), F32),
        ],
    )(prompt_lengths, decode_slot, staying, decay_log[None, :], skip_gain[None, :])


def scan_kernel(heads, width, meta, x_ref, b_ref, c_ref, dt_ref, gain_ref, *rest):
    layer_ref, tail_ref, kept_ref, send_ref, state, out = rest[-6:]
    slot = pl.program_id(0)
    length, filled, before, stay = meta[0], meta[1], meta[2], meta[3]

    @pl.when(slot == 0)
    def _():
        state[...] = jnp.zeros_like(state)

    @pl.when(slot < filled)
    def _():
        first = slot * TILE
        row_ids = lax.broadcasted_iota(jnp.int32, (TILE, TILE), 0)
        col_ids = lax.broadcasted_iota(jnp.int32, (TILE, TILE), 1)
        live_cols = lax.broadcasted_iota(jnp.int32, (1, TILE), 1) + first < length
        live_rows = row_ids + first < length
        step = jnp.where(live_cols, dt_ref[...].astype(F32), 0.0)
        upper = jnp.where(row_ids <= col_ids, 1.0, 0.0).astype(BF16)
        total = jnp.dot(step.astype(BF16), upper, preferred_element_type=F32)
        decay = total * gain_ref[0]
        decay_t = decay.T
        end = decay[:, TILE - 1 : TILE]
        to_end = jnp.exp2(end - decay) * step
        offset = decay - jnp.log2(step)
        b = b_ref[...]
        c = c_ref[...]
        scores = lax.dot_general(c, b, (((1,), (1,)), ((), ())), preferred_element_type=F32)
        scores = jnp.where(row_ids >= col_ids, scores, 0.0)
        b_t = b.astype(F32).T
        left = col_ids < width
        for pair in range(heads // 2):
            cols = pl.ds(pair * TILE, TILE)
            mix, weighted, decay_col = [], [], []
            for h in (2 * pair, 2 * pair + 1):
                column = jnp.broadcast_to(decay_t[:, h : h + 1], (TILE, TILE))
                gap = jnp.minimum(column - offset[h : h + 1, :], CEILING)
                mix.append((jnp.exp2(gap) * scores).astype(BF16))
                weighted.append((b_t * to_end[h : h + 1, :]).astype(BF16))
                decay_col.append(column)
            lhs = jnp.concatenate(
                [jnp.concatenate(mix, axis=1), jnp.concatenate(weighted, axis=1)], axis=0
            )
            x = x_ref[:, cols]
            zero = jnp.zeros_like(x)
            rhs = jnp.concatenate([jnp.where(left, x, zero), jnp.where(left, zero, x)], axis=0)
            both = jnp.dot(lhs, rhs, preferred_element_type=F32)
            held = state[:, cols]
            carried = jnp.dot(c, held.astype(BF16), preferred_element_type=F32)
            growth = jnp.exp2(jnp.where(left, decay_col[0], decay_col[1]))
            skip = jnp.where(
                left[:1], gain_ref[1, 2 * pair : 2 * pair + 1, :], gain_ref[1, 2 * pair + 1 : 2 * pair + 2, :]
            )
            result = both[:TILE] + carried * growth + skip * x.astype(F32)
            out[:, cols] = jnp.where(live_rows, result, 0.0).astype(BF16)
            shrink = growth[TILE - 1 : TILE, :]
            state[:, cols] = shrink * held + both[TILE:]

        @pl.when(slot < W - before)
        def _():
            layer_ref[...] = out[...]

        @pl.when(slot >= W - before)
        def _():
            tail_ref[...] = out[...]

        @pl.when(slot == filled - 1)
        def _():
            keep = stay == 1
            for pair in range(heads // 2):
                cols = pl.ds(pair * TILE, TILE)
                final = state[:, cols].T
                kept_ref[cols, :] = jnp.where(keep, final, 0.0)
                send_ref[cols, :] = final.astype(BF16)


def run_chunk(chunk, chunks, meta, x_rows, b_rows, c_rows, time_step, gains, carry):
    head_count = time_step.shape[0]
    heads = head_count // chunks
    columns = x_rows.shape[1]
    width = columns // head_count
    span = columns // chunks
    last = lambda s, m: jnp.minimum(s, m[1] - 1)
    in_specs = [
        pl.BlockSpec((TILE, span), lambda s, m: (last(s, m), chunk)),
        pl.BlockSpec((TILE, N), lambda s, m: (last(s, m), chunk)),
        pl.BlockSpec((TILE, N), lambda s, m: (last(s, m), chunk)),
        pl.BlockSpec((heads, TILE), lambda s, m: (chunk, last(s, m))),
        pl.BlockSpec((2, heads, TILE), lambda s, m: (0, chunk, 0)),
    ]
    aliases = {}
    extra = ()
    if carry is not None:
        extra = carry
        in_specs += [pl.BlockSpec(memory_space=pl.ANY)] * 3
        aliases = {6: 0, 7: 2, 8: 3}
    grid_spec = pltpu.PrefetchScalarGridSpec(
        num_scalar_prefetch=1,
        grid=(SLOTS,),
        in_specs=in_specs,
        out_specs=[
            pl.BlockSpec((TILE, span), lambda s, m: (jnp.minimum(s + m[2], W - 1), chunk)),
            pl.BlockSpec((TILE, span), lambda s, m: (jnp.clip(s - W + m[2], 0, TAIL - 1), 0)),
            pl.BlockSpec((span, N), lambda s, m: (chunk, 0)),
            pl.BlockSpec((span, N), lambda s, m: (chunk, 0)),
        ],
        scratch_shapes=[pltpu.VMEM((N, span), F32), pltpu.VMEM((TILE, span), BF16)],
    )
    layer, tail, kept, send = pl.pallas_call(
        lambda *refs: scan_kernel(heads, width, *refs),
        grid_spec=grid_spec,
        out_shape=[
            jax.ShapeDtypeStruct((W * TILE, columns), BF16),
            jax.ShapeDtypeStruct((TAIL * TILE, span), BF16),
            jax.ShapeDtypeStruct((columns, N), F32),
            jax.ShapeDtypeStruct((columns, N), BF16),
        ],
        input_output_aliases=aliases,
        compiler_params=pltpu.CompilerParams(vmem_limit_bytes=VMEM),
        cost_estimate=pl.CostEstimate(flops=3 * 10**10, bytes_accessed=8 * 10**6, transcendentals=0),
    )(meta, x_rows, b_rows, c_rows, time_step, gains, *extra)
    return tail, (layer, kept, send)


def place_chunk(chunk, meta, moved, layer, after=()):
    span = moved.shape[1]

    def kernel(meta, moved_ref, *rest):
        layer_ref, sems = rest[-2:]
        copies = []
        for j in range(TAIL):
            rows = pl.ds(j * TILE, TILE)
            target = layer_ref.at[rows, pl.ds(chunk * span, span)]
            copies.append(pltpu.make_async_copy(moved_ref.at[rows, :], target, sems.at[j]))
        for j in range(TAIL):
            pl.when(j < meta[2])(copies[j].start)
        for j in range(TAIL):
            pl.when(j < meta[2])(copies[j].wait)

    return pl.pallas_call(
        kernel,
        grid_spec=pltpu.PrefetchScalarGridSpec(
            num_scalar_prefetch=1,
            grid=(),
            in_specs=[pl.BlockSpec(memory_space=pltpu.VMEM)]
            + [pl.BlockSpec(memory_space=pl.ANY)] * (1 + len(after)),
            out_specs=pl.BlockSpec(memory_space=pl.ANY),
            scratch_shapes=[pltpu.SemaphoreType.DMA((TAIL,))],
        ),
        out_shape=jax.ShapeDtypeStruct(layer.shape, layer.dtype),
        input_output_aliases={2: 0},
        compiler_params=pltpu.CompilerParams(vmem_limit_bytes=VMEM // 8),
        cost_estimate=pl.CostEstimate(flops=3 * 10**10, bytes_accessed=2 * 10**6, transcendentals=0),
    )(meta, moved, layer, *after)


def place_states(source, arrived):
    _, heads, width, entries = arrived.shape

    def kernel(source, arrived_ref, decode_ref):
        have = source[pl.program_id(0)] >= 0
        decode_ref[:, 0] = jnp.where(have, arrived_ref[0].astype(F32), 0.0)

    return pl.pallas_call(
        kernel,
        grid_spec=pltpu.PrefetchScalarGridSpec(
            num_scalar_prefetch=1,
            grid=(DCAP,),
            in_specs=[
                pl.BlockSpec(
                    (1, heads, width, entries), lambda c, src: (jnp.maximum(src[c], 0), 0, 0, 0)
                )
            ],
            out_specs=pl.BlockSpec((heads, 1, width, entries), lambda c, src: (0, c, 0, 0)),
        ),
        out_shape=jax.ShapeDtypeStruct((heads, DCAP, width, entries), F32),
        compiler_params=pltpu.CompilerParams(vmem_limit_bytes=VMEM),
        cost_estimate=pl.CostEstimate(flops=0, bytes_accessed=5 * 10**6, transcendentals=0),
    )(source, arrived)


def body(
    x_rows,
    b_rows,
    c_rows,
    time_step,
    decay_log,
    skip_gain,
    prompt_lengths,
    block_lists,
    decode_slot,
    staying,
):
    head_count = decay_log.shape[0]
    columns = x_rows.shape[1]
    width = columns // head_count
    chunks = b_rows.shape[1] // N
    req_count = lax.axis_size("req")
    meta, source, gains = prepare(prompt_lengths, decode_slot, staying, decay_log, skip_gain)
    carry = None
    moved = []
    for chunk in range(chunks):
        if chunk == 2:
            layer = place_chunk(chunk - 2, meta, moved[chunk - 2], carry[0])
            carry = (layer, carry[1], carry[2])
        tail, carry = run_chunk(
            chunk, chunks, meta, x_rows, b_rows, c_rows, time_step, gains, carry
        )
        moved.append(shifted(tail, "req", 1))
    layer, kept, send = carry
    pieces = send.reshape(DEC_REQ, head_count // DEC_REQ, width, N)
    groups = req_count // DEC_REQ
    outgoing = jnp.concatenate([pieces] * groups, axis=0) if groups > 1 else pieces
    arrived = lax.all_to_all(outgoing, "req", split_axis=0, concat_axis=0, tiled=True)
    decoded = place_states(source, arrived)
    for chunk in range(1, chunks):
        after = (decoded,) if chunk == chunks - 1 else ()
        layer = place_chunk(chunk, meta, moved[chunk], layer, after)
    return (layer, kept.reshape(1, head_count, width, N), decoded[None, None])


def solution(mesh):
    placed = (
        P(("grp", "req"), "head"),
        P(("grp", "req"), "head"),
        P(("grp", "req"), "head"),
        P("head", ("grp", "req")),
        P("head"),
        P("head"),
        P("grp"),
        P("grp", None),
        P("grp"),
        P("grp"),
    )
    return jax.shard_map(
        body,
        mesh=mesh,
        in_specs=placed,
        out_specs=(
            P(("grp", "req"), "head"),
            P(("grp", "req"), "head", None, None),
            P(("grp", "req"), "head", None, None, None, None),
        ),
        check_vma=False,
    )
```

profile of v0, /device:TPU:18, one launch (start us, length us, event | category | flops | bytes accessed | tf_op | source)
XLA Modules:
  0.0 176.8 jit_solution(17281395015972891068)
XLA Ops:
  0.6 1.5 shard_map.112
  2.1 11.3 %shard_map.113 = (bf16[768,4096]{1,0:T(8,128)(2,1)}, bf16[640,1024]{1,0:T(8,128)(2,1)}, f32[4096,128]{1,0:T(8,128)}, bf16[4096,128]{1,0:T(8,128)(2,1)}) custom-call(s32[4]{0:T(128)} %get-tuple-element.22.refs_0_.meta, bf16[1408,4096]{1,0:T(8,128)(2,1)} %refs_1_.7, bf16[1408,512]{1,0:T(8,128)(2,1)} %refs_2_.7, bf16[1408,512]{1,0:T(8,128)(2,1)} %refs_3_.7, ...), custom_call_target="tpu_custom_call" | custom-call | flops 30000001024 | bytes 8000000 | tf_op jit(solution)/shard_map/pallas_call | solution.py:175
  13.4 1.9 %collective-permute-start = (bf16[640,1024]{1,0:T(8,128)(2,1)}, bf16[640,1024]{1,0:T(8,128)(2,1)S(1)}, u32[]{:S(2)}, u32[]{:S(2)}) collective-permute-start(bf16[640,1024]{1,0:T(8,128)(2,1)} %get-tuple-element.24), channel_id=1, source_target_pairs={{0,2},{2,4},{4,6},{6,8},{8,10},{10,12},{12,14},{1,3},{3,5},{5,7},{... | collective-permute-start | bytes 3932168 | tf_op jit(solution)/shard_map/ppermute | solution.py:27
  15.3 0.0 copy-start.1
  15.4 11.4 %shard_map.114 = (bf16[768,4096]{1,0:T(8,128)(2,1)}, bf16[640,1024]{1,0:T(8,128)(2,1)}, f32[4096,128]{1,0:T(8,128)}, bf16[4096,128]{1,0:T(8,128)(2,1)}) custom-call(s32[4]{0:T(128)} %get-tuple-element.22.refs_0_.meta, bf16[1408,4096]{1,0:T(8,128)(2,1)} %refs_1_.7, ...), custom_call_target="tpu_custom_call", output_to_operand_aliasing={{0}: (6, {}), {2}: (7, {}), {3}: (8, {})} | custom-call | flops 30000001024 | bytes 8000000 | tf_op jit(solution)/shard_map/pallas_call | solution.py:175
  26.7 3.6 %collective-permute-start.3 = (bf16[640,1024]{1,0:T(8,128)(2,1)}, bf16[640,1024]{1,0:T(8,128)(2,1)S(1)}, u32[]{:S(2)}, u32[]{:S(2)}) collective-permute-start(bf16[640,1024]{1,0:T(8,128)(2,1)} %get-tuple-element.36), channel_id=1, source_target_pairs={{0,2},{2,4},{4,6},{6,8},{8,10},{10,12},{12,14},{1,3},{3,5},{5,7},{... | collective-permute-start | bytes 3932168 | tf_op jit(solution)/shard_map/ppermute | solution.py:27
  30.4 17.7 %collective-permute-done.moved_ref = bf16[640,1024]{1,0:T(8,128)(2,1)S(1)} collective-permute-done((bf16[640,1024]{1,0:T(8,128)(2,1)}, bf16[640,1024]{1,0:T(8,128)(2,1)S(1)}, u32[]{:S(2)}, u32[]{:S(2)}) %collective-permute-start) | collective-permute-done | bytes 1310752 | tf_op jit(solution)/shard_map/ppermute | solution.py:27
  48.1 0.0 copy-done.1
  48.1 1.5 shard_map.115.refs_6_
  49.6 11.3 %shard_map.116 = (bf16[768,4096]{1,0:T(8,128)(2,1)}, bf16[640,1024]{1,0:T(8,128)(2,1)}, f32[4096,128]{1,0:T(8,128)}, bf16[4096,128]{1,0:T(8,128)(2,1)}) custom-call(s32[4]{0:T(128)} %get-tuple-element.22.refs_0_.meta, bf16[1408,4096]{1,0:T(8,128)(2,1)} %refs_1_.7, ...), custom_call_target="tpu_custom_call", output_to_operand_aliasing={{0}: (6, {}), {2}: (7, {}), {3}: (8, {})} | custom-call | flops 30000001024 | bytes 8000000 | tf_op jit(solution)/shard_map/pallas_call | solution.py:175
  60.9 11.3 %shard_map.117 = (bf16[768,4096]{1,0:T(8,128)(2,1)}, bf16[640,1024]{1,0:T(8,128)(2,1)}, f32[4096,128]{1,0:T(8,128)}, bf16[4096,128]{1,0:T(8,128)(2,1)}) custom-call(s32[4]{0:T(128)} %get-tuple-element.22.refs_0_.meta, bf16[1408,4096]{1,0:T(8,128)(2,1)} %refs_1_.7, ...), custom_call_target="tpu_custom_call", output_to_operand_aliasing={{0}: (6, {}), {2}: (7, {}), {3}: (8, {})} | custom-call | flops 30000001024 | bytes 8000000 | tf_op jit(solution)/shard_map/pallas_call | solution.py:175
  72.2 0.0 copy-start.2
  72.2 13.5 %all-to-all-start = ((bf16[8,8,64,128]{3,2,1,0:T(8,128)(2,1)}), bf16[8,8,64,128]{3,2,1,0:T(8,128)(2,1)}, u32[]{:S(2)}, u32[]{:S(2)}) async-start(bf16[8,8,64,128]{3,2,1,0:T(8,128)(2,1)} %bitcast.6), calls=%async_computation | async-start | bytes 2097152 | tf_op jit(solution)/shard_map/all_to_all | solution.py:280
  85.7 3.4 %collective-permute-start.1 = (bf16[640,1024]{1,0:T(8,128)(2,1)}, bf16[640,1024]{1,0:T(8,128)(2,1)S(1)}, u32[]{:S(2)}, u32[]{:S(2)}) collective-permute-start(bf16[640,1024]{1,0:T(8,128)(2,1)} %get-tuple-element.34), channel_id=1, source_target_pairs={{0,2},{2,4},{4,6},{6,8},{8,10},{10,12},{12,14},{1,3},{3,5},{5,7},{... | collective-permute-start | bytes 3932168 | tf_op jit(solution)/shard_map/ppermute | solution.py:27
  89.1 3.4 %collective-permute-start.2 = (bf16[640,1024]{1,0:T(8,128)(2,1)}, bf16[640,1024]{1,0:T(8,128)(2,1)S(1)}, u32[]{:S(2)}, u32[]{:S(2)}) collective-permute-start(bf16[640,1024]{1,0:T(8,128)(2,1)} %get-tuple-element.35), channel_id=1, source_target_pairs={{0,2},{2,4},{4,6},{6,8},{8,10},{10,12},{12,14},{1,3},{3,5},{5,7},{... | collective-permute-start | bytes 3932168 | tf_op jit(solution)/shard_map/ppermute | solution.py:27
  92.5 0.0 collective-permute-done.3.moved_ref
  92.5 0.0 copy-done.2
  92.5 1.5 shard_map.118.rest_0_
  94.0 70.3 %collective-permute-done.2.moved_ref = bf16[640,1024]{1,0:T(8,128)(2,1)S(1)} collective-permute-done((bf16[640,1024]{1,0:T(8,128)(2,1)}, bf16[640,1024]{1,0:T(8,128)(2,1)S(1)}, u32[]{:S(2)}, u32[]{:S(2)}) %collective-permute-start.2) | collective-permute-done | bytes 1310752 | tf_op jit(solution)/shard_map/ppermute | solution.py:27
  164.2 1.5 shard_map.119.rest_0_
  165.7 0.0 all-to-all-done.arrived_ref
  165.7 7.7 %shard_map.120.rest_1_ = f32[8,12,64,128]{3,2,1,0:T(8,128)} custom-call(s32[12]{0:T(128)} %get-tuple-element.38.source, bf16[8,8,64,128]{3,2,1,0:T(8,128)(2,1)} %all-to-all-done.arrived_ref), custom_call_target="tpu_custom_call" | custom-call | bytes 5000000 | tf_op jit(solution)/shard_map/pallas_call | solution.py:230
  173.4 0.0 collective-permute-done.1.moved_ref
  173.4 0.0 copy-start
  173.4 1.9 %copy-done = f32[8,12,64,128]{3,2,1,0:T(8,128)S(1)} copy-done((f32[8,12,64,128]{3,2,1,0:T(8,128)S(1)}, f32[8,12,64,128]{3,2,1,0:T(8,128)}, u32[]{:S(2)}) %copy-start) | copy-done | bytes 3145752
  175.3 1.5 shard_map.121
Async XLA Ops:
  13.4 34.7 %collective-permute-start = (bf16[640,1024]{1,0:T(8,128)(2,1)}, bf16[640,1024]{1,0:T(8,128)(2,1)S(1)}, u32[]{:S(2)}, u32[]{:S(2)}) collective-permute-start(bf16[640,1024]{1,0:T(8,128)(2,1)} %get-tuple-element.24), channel_id=1, source_target_pairs={{0,2},{2,4},{4,6},{6,8},{8,10},{10,12},{12,14},{1,3},{3,5},{5,7},{... | collective-permute-start | bytes 3932168 | tf_op jit(solution)/shard_map/ppermute | solution.py:27
  15.3 32.7 %copy-start.1 = (s32[4]{0:T(128)S(1)}, s32[4]{0:T(128)}, u32[]{:S(2)}) copy-start(s32[4]{0:T(128)} %get-tuple-element.22.refs_0_.meta) | copy-start | bytes 52
  26.7 65.7 %collective-permute-start.3 = (bf16[640,1024]{1,0:T(8,128)(2,1)}, bf16[640,1024]{1,0:T(8,128)(2,1)S(1)}, u32[]{:S(2)}, u32[]{:S(2)}) collective-permute-start(bf16[640,1024]{1,0:T(8,128)(2,1)} %get-tuple-element.36), channel_id=1, source_target_pairs={{0,2},{2,4},{4,6},{6,8},{8,10},{10,12},{12,14},{1,3},{3,5},{5,7},{... | collective-permute-start | bytes 3932168 | tf_op jit(solution)/shard_map/ppermute | solution.py:27
  72.2 20.3 %copy-start.2 = (s32[4]{0:T(128)S(1)}, s32[4]{0:T(128)}, u32[]{:S(2)}) copy-start(s32[4]{0:T(128)} %get-tuple-element.22.refs_0_.meta) | copy-start | bytes 52
  72.2 93.5 %all-to-all-start = ((bf16[8,8,64,128]{3,2,1,0:T(8,128)(2,1)}), bf16[8,8,64,128]{3,2,1,0:T(8,128)(2,1)}, u32[]{:S(2)}, u32[]{:S(2)}) async-start(bf16[8,8,64,128]{3,2,1,0:T(8,128)(2,1)} %bitcast.6), calls=%async_computation | async-start | bytes 2097152 | tf_op jit(solution)/shard_map/all_to_all | solution.py:280
  85.7 87.7 %collective-permute-start.1 = (bf16[640,1024]{1,0:T(8,128)(2,1)}, bf16[640,1024]{1,0:T(8,128)(2,1)S(1)}, u32[]{:S(2)}, u32[]{:S(2)}) collective-permute-start(bf16[640,1024]{1,0:T(8,128)(2,1)} %get-tuple-element.34), channel_id=1, source_target_pairs={{0,2},{2,4},{4,6},{6,8},{8,10},{10,12},{12,14},{1,3},{3,5},{5,7},{... | collective-permute-start | bytes 3932168 | tf_op jit(solution)/shard_map/ppermute | solution.py:27
  89.1 75.1 %collective-permute-start.2 = (bf16[640,1024]{1,0:T(8,128)(2,1)}, bf16[640,1024]{1,0:T(8,128)(2,1)S(1)}, u32[]{:S(2)}, u32[]{:S(2)}) collective-permute-start(bf16[640,1024]{1,0:T(8,128)(2,1)} %get-tuple-element.35), channel_id=1, source_target_pairs={{0,2},{2,4},{4,6},{6,8},{8,10},{10,12},{12,14},{1,3},{3,5},{5,7},{... | collective-permute-start | bytes 3932168 | tf_op jit(solution)/shard_map/ppermute | solution.py:27
  173.4 1.9 %copy-start = (f32[8,12,64,128]{3,2,1,0:T(8,128)S(1)}, f32[8,12,64,128]{3,2,1,0:T(8,128)}, u32[]{:S(2)}) copy-start(f32[8,12,64,128]{3,2,1,0:T(8,128)} %shard_map.120.rest_1_) | copy-start | bytes 9437188
where the time goes:
time: 178 us; the launch traced here: 177 us
  waiting for transfers between devices  88 us (49%)
  Pallas kernels  60.4 us (34%)
  starting transfers between devices  25.8 us (14%)
  local copies, waits for them, and re-layouts  1.9 us (1%)
    ppermute x4, waiting for transfers between devices, shifted(): return lax.ppermute(block, axis, route)  88 us
    pallas_call x4, Pallas kernels, run_chunk(): pl.pallas_call(lambda *refs: scan_kernel(heads, width, *refs), grid_spec=...  45.3 us
    all_to_all x1, starting transfers between devices, body(): lax.all_to_all(outgoing, 'req', split_axis=0, concat_axis=0, tiled=True)  13.5 us
    ppermute x4, starting transfers between devices, shifted(): return lax.ppermute(block, axis, route)  12.3 us
    pallas_call x1, Pallas kernels, place_states(): pl.pallas_call(kernel, grid_spec=pltpu.PrefetchScalarGridSpec(num_scalar_...  7.68 us
    pallas_call x4, Pallas kernels, place_chunk(): pl.pallas_call(kernel, grid_spec=pltpu.PrefetchScalarGridSpec(num_scalar_...  5.85 us
  transfers between devices with their start and end apart: 5, of which 2 were waited for; matrix products, arithmetic and copies ran while one was open for 0% of the time, Pallas kernels for 26%

commit v1 on v0

--- a/solution.py
+++ b/solution.py
@@ -65,38 +65,84 @@
     )(prompt_lengths, decode_slot, staying, decay_log[None, :], skip_gain[None, :])
 
 
-def scan_kernel(heads, width, meta, x_ref, b_ref, c_ref, dt_ref, gain_ref, *rest):
-    layer_ref, tail_ref, kept_ref, send_ref, state, out = rest[-6:]
-    slot = pl.program_id(0)
+def scan_kernel(start, groups, heads, width, meta, x_hbm, b_hbm, c_hbm, dt_hbm, gain_ref, *rest):
+    outputs = rest[-16 - groups : -13]
+    layer_hbm, kept_hbm, send_hbm = outputs[:3]
+    tails_hbm = outputs[3:]
+    (xs, bs, cs, dts, outs, state, kept, send, rows_d, cols_d, in_sems, out_sems, end_sems) = rest[-13:]
     length, filled, before, stay = meta[0], meta[1], meta[2], meta[3]
-
-    @pl.when(slot == 0)
-    def _():
-        state[...] = jnp.zeros_like(state)
-
-    @pl.when(slot < filled)
-    def _():
-        first = slot * TILE
-        row_ids = lax.broadcasted_iota(jnp.int32, (TILE, TILE), 0)
-        col_ids = lax.broadcasted_iota(jnp.int32, (TILE, TILE), 1)
-        live_cols = lax.broadcasted_iota(jnp.int32, (1, TILE), 1) + first < length
-        live_rows = row_ids + first < length
-        step = jnp.where(live_cols, dt_ref[...].astype(F32), 0.0)
-        upper = jnp.where(row_ids <= col_ids, 1.0, 0.0).astype(BF16)
+    span = xs.shape[2]
+    part = span // groups
+    per_group = heads // groups
+    wide = pl.ds(start * part, span)
+    narrow = pl.ds(start * N, groups * N)
+
+    def block(slot):
+        return pl.ds(pl.multiple_of(slot * TILE, TILE), TILE)
+
+    def fetches(slot):
+        return [
+            pltpu.make_async_copy(c_hbm.at[block(slot), narrow], cs.at[slot], in_sems.at[0, slot]),
+            pltpu.make_async_copy(b_hbm.at[block(slot), narrow], bs.at[slot], in_sems.at[1, slot]),
+            pltpu.make_async_copy(x_hbm.at[block(slot), wide], xs.at[slot], in_sems.at[2, slot]),
+        ]
+
+    def to_layer(slot):
+        target = layer_hbm.at[block(slot + before), wide]
+        return [pltpu.make_async_copy(outs.at[slot], target, out_sems.at[0, slot])]
+
+    def to_tail(slot):
+        copies = []
+        for g in range(groups):
+            target = tails_hbm[g].at[block(slot - W + before)]
+            source = outs.at[slot, :, pl.ds(g * part, part)]
+            copies.append(pltpu.make_async_copy(source, target, out_sems.at[1 + g, slot]))
+        return copies
+
+    steps = pltpu.make_async_copy(
+        dt_hbm.at[pl.ds(start * per_group, heads), :], dts, end_sems.at[0]
+    )
+    steps.start()
+    for slot in range(SLOTS):
+
+        @pl.when(slot < filled)
+        def _():
+            for copy in fetches(slot):
+                copy.start()
+
+    state[...] = jnp.zeros_like(state)
+    row_ids = lax.broadcasted_iota(jnp.int32, (TILE, TILE), 0)
+    col_ids = lax.broadcasted_iota(jnp.int32, (TILE, TILE), 1)
+    left = col_ids < width
+    upper = jnp.where(row_ids <= col_ids, 1.0, 0.0).astype(BF16)
+    rate = gain_ref[0, start * per_group : start * per_group + heads, :]
+    steps.wait()
+    for slot in range(SLOTS):
+        live = lax.broadcasted_iota(jnp.int32, (1, TILE), 1) + slot * TILE < length
+        step = jnp.where(live, dts[:, slot * TILE : (slot + 1) * TILE].astype(F32), 0.0)
         total = jnp.dot(step.astype(BF16), upper, preferred_element_type=F32)
-        decay = total * gain_ref[0]
-        decay_t = decay.T
-        end = decay[:, TILE - 1 : TILE]
-        to_end = jnp.exp2(end - decay) * step
-        offset = decay - jnp.log2(step)
-        b = b_ref[...]
-        c = c_ref[...]
-        scores = lax.dot_general(c, b, (((1,), (1,)), ((), ())), preferred_element_type=F32)
-        scores = jnp.where(row_ids >= col_ids, scores, 0.0)
-        b_t = b.astype(F32).T
-        left = col_ids < width
+        decay = total * rate
+        rows_d[slot, 0] = decay - jnp.log2(step)
+        rows_d[slot, 1] = jnp.exp2(decay[:, TILE - 1 : TILE] - decay) * step
+        cols_d[slot] = decay.T
+
+    def advance(slot, _):
+        for copy in fetches(slot):
+            copy.wait()
+        live_rows = row_ids + slot * TILE < length
+        shared = []
+        for g in range(groups):
+            b = bs[slot, :, g * N : (g + 1) * N]
+            c = cs[slot, :, g * N : (g + 1) * N]
+            scores = lax.dot_general(c, b, (((1,), (1,)), ((), ())), preferred_element_type=F32)
+            scores = jnp.where(row_ids >= col_ids, scores, 0.0)
+            shared.append((c, scores, b.astype(F32).T))
+        offset = rows_d[slot, 0]
+        to_end = rows_d[slot, 1]
+        decay_t = cols_d[slot]
         for pair in range(heads // 2):
             cols = pl.ds(pair * TILE, TILE)
+            c, scores, b_t = shared[2 * pair // per_group]
             mix, weighted, decay_col = [], [], []
             for h in (2 * pair, 2 * pair + 1):
                 column = jnp.broadcast_to(decay_t[:, h : h + 1], (TILE, TILE))
@@ -107,85 +153,116 @@
             lhs = jnp.concatenate(
                 [jnp.concatenate(mix, axis=1), jnp.concatenate(weighted, axis=1)], axis=0
             )
-            x = x_ref[:, cols]
+            x = xs[slot, :, cols]
             zero = jnp.zeros_like(x)
             rhs = jnp.concatenate([jnp.where(left, x, zero), jnp.where(left, zero, x)], axis=0)
             both = jnp.dot(lhs, rhs, preferred_element_type=F32)
             held = state[:, cols]
             carried = jnp.dot(c, held.astype(BF16), preferred_element_type=F32)
             growth = jnp.exp2(jnp.where(left, decay_col[0], decay_col[1]))
+            first = start * per_group + 2 * pair
             skip = jnp.where(
-                left[:1], gain_ref[1, 2 * pair : 2 * pair + 1, :], gain_ref[1, 2 * pair + 1 : 2 * pair + 2, :]
+                left[:1], gain_ref[1, first : first + 1, :], gain_ref[1, first + 1 : first + 2, :]
             )
             result = both[:TILE] + carried * growth + skip * x.astype(F32)
-            out[:, cols] = jnp.where(live_rows, result, 0.0).astype(BF16)
+            outs[slot, :, cols] = jnp.where(live_rows, result, 0.0).astype(BF16)
             shrink = growth[TILE - 1 : TILE, :]
             state[:, cols] = shrink * held + both[TILE:]
 
         @pl.when(slot < W - before)
         def _():
-            layer_ref[...] = out[...]
+            for copy in to_layer(slot):
+                copy.start()
 
         @pl.when(slot >= W - before)
         def _():
-            tail_ref[...] = out[...]
-
-        @pl.when(slot == filled - 1)
-        def _():
-            keep = stay == 1
-            for pair in range(heads // 2):
-                cols = pl.ds(pair * TILE, TILE)
-                final = state[:, cols].T
-                kept_ref[cols, :] = jnp.where(keep, final, 0.0)
-                send_ref[cols, :] = final.astype(BF16)
-
-
-def run_chunk(chunk, chunks, meta, x_rows, b_rows, c_rows, time_step, gains, carry):
+            for copy in to_tail(slot):
+                copy.start()
+
+        return 0
+
+    lax.fori_loop(0, filled, advance, 0)
+    keep = stay == 1
+    for pair in range(heads // 2):
+        cols = pl.ds(pair * TILE, TILE)
+        final = state[:, cols].T
+        kept[cols, :] = jnp.where(keep, final, 0.0)
+        send[cols, :] = final.astype(BF16)
+    last = [
+        pltpu.make_async_copy(kept, kept_hbm.at[wide], end_sems.at[1]),
+        pltpu.make_async_copy(send, send_hbm.at[wide], end_sems.at[2]),
+    ]
+    for copy in last:
+        copy.start()
+
+    def drain(slot, _):
+        @pl.when(slot < W - before)
+        def _():
+            for copy in to_layer(slot):
+                copy.wait()
+
+        @pl.when(slot >= W - before)
+        def _():
+            for copy in to_tail(slot):
+                copy.wait()
+
+        return 0
+
+    lax.fori_loop(0, filled, drain, 0)
+    for copy in last:
+        copy.wait()
+
+
+def run_groups(start, groups, total, meta, x_rows, b_rows, c_rows, time_step, gains, carry):
     head_count = time_step.shape[0]
-    heads = head_count // chunks
+    heads = head_count // total * groups
     columns = x_rows.shape[1]
     width = columns // head_count
-    span = columns // chunks
-    last = lambda s, m: jnp.minimum(s, m[1] - 1)
-    in_specs = [
-        pl.BlockSpec((TILE, span), lambda s, m: (last(s, m), chunk)),
-        pl.BlockSpec((TILE, N), lambda s, m: (last(s, m), chunk)),
-        pl.BlockSpec((TILE, N), lambda s, m: (last(s, m), chunk)),
-        pl.BlockSpec((heads, TILE), lambda s, m: (chunk, last(s, m))),
-        pl.BlockSpec((2, heads, TILE), lambda s, m: (0, chunk, 0)),
-    ]
+    part = columns // total
+    span = part * groups
+    whole = pl.BlockSpec(memory_space=pl.ANY)
+    in_specs = [whole] * 4 + [pl.BlockSpec(memory_space=pltpu.VMEM)]
     aliases = {}
     extra = ()
     if carry is not None:
         extra = carry
-        in_specs += [pl.BlockSpec(memory_space=pl.ANY)] * 3
-        aliases = {6: 0, 7: 2, 8: 3}
+        in_specs += [whole] * 3
+        aliases = {6: 0, 7: 1, 8: 2}
     grid_spec = pltpu.PrefetchScalarGridSpec(
         num_scalar_prefetch=1,
-        grid=(SLOTS,),
+        grid=(),
         in_specs=in_specs,
-        out_specs=[
-            pl.BlockSpec((TILE, span), lambda s, m: (jnp.minimum(s + m[2], W - 1), chunk)),
-            pl.BlockSpec((TILE, span), lambda s, m: (jnp.clip(s - W + m[2], 0, TAIL - 1), 0)),
-            pl.BlockSpec((span, N), lambda s, m: (chunk, 0)),
-            pl.BlockSpec((span, N), lambda s, m: (chunk, 0)),
+        out_specs=[whole] * (3 + groups),
+        scratch_shapes=[
+            pltpu.VMEM((SLOTS, TILE, span), BF16),
+            pltpu.VMEM((SLOTS, TILE, groups * N), BF16),
+            pltpu.VMEM((SLOTS, TILE, groups * N), BF16),
+            pltpu.VMEM((heads, SLOTS * TILE), BF16),
+            pltpu.VMEM((SLOTS, TILE, span), BF16),
+            pltpu.VMEM((N, span), F32),
+            pltpu.VMEM((span, N), F32),
+            pltpu.VMEM((span, N), BF16),
+            pltpu.VMEM((SLOTS, 2, heads, TILE), F32),
+            pltpu.VMEM((SLOTS, TILE, heads), F32),
+            pltpu.SemaphoreType.DMA((3, SLOTS)),
+            pltpu.SemaphoreType.DMA((1 + groups, SLOTS)),
+            pltpu.SemaphoreType.DMA((3,)),
         ],
-        scratch_shapes=[pltpu.VMEM((N, span), F32), pltpu.VMEM((TILE, span), BF16)],
     )
-    layer, tail, kept, send = pl.pallas_call(
-        lambda *refs: scan_kernel(heads, width, *refs),
+    layer, kept, send, *tails = pl.pallas_call(
+        lambda *refs: scan_kernel(start, groups, heads, width, *refs),
         grid_spec=grid_spec,
         out_shape=[
             jax.ShapeDtypeStruct((W * TILE, columns), BF16),
-            jax.ShapeDtypeStruct((TAIL * TILE, span), BF16),
             jax.ShapeDtypeStruct((columns, N), F32),
             jax.ShapeDtypeStruct((columns, N), BF16),
-        ],
+        ]
+        + [jax.ShapeDtypeStruct((TAIL * TILE, part), BF16)] * groups,
         input_output_aliases=aliases,
         compiler_params=pltpu.CompilerParams(vmem_limit_bytes=VMEM),
         cost_estimate=pl.CostEstimate(flops=3 * 10**10, bytes_accessed=8 * 10**6, transcendentals=0),
     )(meta, x_rows, b_rows, c_rows, time_step, gains, *extra)
-    return tail, (layer, kept, send)
+    return tails, (layer, kept, send)
 
 
 def place_chunk(chunk, meta, moved, layer, after=()):
@@ -263,24 +340,21 @@
     chunks = b_rows.shape[1] // N
     req_count = lax.axis_size("req")
     meta, source, gains = prepare(prompt_lengths, decode_slot, staying, decay_log, skip_gain)
+    moved = []
     carry = None
-    moved = []
-    for chunk in range(chunks):
-        if chunk == 2:
-            layer = place_chunk(chunk - 2, meta, moved[chunk - 2], carry[0])
-            carry = (layer, carry[1], carry[2])
-        tail, carry = run_chunk(
-            chunk, chunks, meta, x_rows, b_rows, c_rows, time_step, gains, carry
+    for start, groups in ((0, 1), (1, chunks - 1)):
+        tails, carry = run_groups(
+            start, groups, chunks, meta, x_rows, b_rows, c_rows, time_step, gains, carry
         )
-        moved.append(shifted(tail, "req", 1))
+        moved += [shifted(tail, "req", 1) for tail in tails]
     layer, kept, send = carry
     pieces = send.reshape(DEC_REQ, head_count // DEC_REQ, width, N)
     groups = req_count // DEC_REQ
     outgoing = jnp.concatenate([pieces] * groups, axis=0) if groups > 1 else pieces
     arrived = lax.all_to_all(outgoing, "req", split_axis=0, concat_axis=0, tiled=True)
     decoded = place_states(source, arrived)
-    for chunk in range(1, chunks):
-        after = (decoded,) if chunk == chunks - 1 else ()
+    for chunk in range(chunks):
+        after = (decoded,) if chunk == 1 else ()
         layer = place_chunk(chunk, meta, moved[chunk], layer, after)
     return (layer, kept.reshape(1, head_count, width, N), decoded[None, None])
 

time: 178 us -> 174 us (0.978)
  Pallas kernels: 60.4 us -> 44.9 us
  starting transfers between devices: 25.8 us -> 33.7 us
  waiting for transfers between devices: 88 us -> 89.9 us
    pallas_call x4 -> x2, Pallas kernels: 45.3 us -> 30.4 us  [run_groups(): pl.pallas_call(lambda *refs: scan_kernel(start, groups, heads, width, *re...]
    all_to_all x1, waiting for transfers between devices: 0.01 us -> 11.7 us  [body(): lax.all_to_all(outgoing, 'req', split_axis=0, concat_axis=0, tiled=True)]
    ppermute x4, waiting for transfers between devices: 88 us -> 78.2 us  [shifted(): return lax.ppermute(block, axis, route)]
    ppermute x4, starting transfers between devices: 12.3 us -> 18 us  [shifted(): return lax.ppermute(block, axis, route)]
    all_to_all x1, starting transfers between devices: 13.5 us -> 15.7 us  [body(): lax.all_to_all(outgoing, 'req', split_axis=0, concat_axis=0, tiled=True)]
  transfers between devices with their start and end apart: 5 -> 5, of which waited for: 2 -> 2; matrix products, arithmetic and copies ran while one was open for 0% -> 0% of each run, Pallas kernels for 26% -> 19%
where the time goes in v1:
time: 174 us; the launch traced here: 171 us
  waiting for transfers between devices  89.9 us (52%)
  Pallas kernels  44.9 us (26%)
  starting transfers between devices  33.7 us (19%)
  local copies, waits for them, and re-layouts  1.89 us (1%)
    ppermute x4, waiting for transfers between devices, shifted(): return lax.ppermute(block, axis, route)  78.2 us
    pallas_call x2, Pallas kernels, run_groups(): pl.pallas_call(lambda *refs: scan_kernel(start, groups, heads, width, *re...  30.4 us
    ppermute x4, starting transfers between devices, shifted(): return lax.ppermute(block, axis, route)  18 us
    all_to_all x1, starting transfers between devices, body(): lax.all_to_all(outgoing, 'req', split_axis=0, concat_axis=0, tiled=True)  15.7 us
    all_to_all x1, waiting for transfers between devices, body(): lax.all_to_all(outgoing, 'req', split_axis=0, concat_axis=0, tiled=True)  11.7 us
    pallas_call x1, Pallas kernels, place_states(): pl.pallas_call(kernel, grid_spec=pltpu.PrefetchScalarGridSpec(num_scalar_...  8 us
    pallas_call x4, Pallas kernels, place_chunk(): pl.pallas_call(kernel, grid_spec=pltpu.PrefetchScalarGridSpec(num_scalar_...  5.04 us
  transfers between devices with their start and end apart: 5, of which 2 were waited for; matrix products, arithmetic and copies ran while one was open for 0% of the time, Pallas kernels for 19%

profile of v1, /device:TPU:18, one launch (start us, length us, event | category | flops | bytes accessed | tf_op | source)
XLA Modules:
  0.0 171.2 jit_solution(12374421152921426627)
XLA Ops:
  0.6 1.5 shard_map.112
  2.1 9.9 %shard_map.113 = (bf16[768,4096]{1,0:T(8,128)(2,1)}, f32[4096,128]{1,0:T(8,128)}, bf16[4096,128]{1,0:T(8,128)(2,1)}, bf16[640,1024]{1,0:T(8,128)(2,1)}) custom-call(s32[4]{0:T(128)} %get-tuple-element.16.refs_0_.meta, bf16[1408,4096]{1,0:T(8,128)(2,1)} %refs_1_.3, bf16[1408,512]{1,0:T(8,128)(2,1)} %refs_2_.3, bf16[1408,512]{1,0:T(8,128)(2,1)} %refs_3_.3, ...), custom_call_target="tpu_custom_call" | custom-call | flops 30000001024 | bytes 8000000 | tf_op jit(solution)/shard_map/pallas_call | solution.py:252
  12.0 7.9 %collective-permute-start.3 = (bf16[640,1024]{1,0:T(8,128)(2,1)}, bf16[640,1024]{1,0:T(8,128)(2,1)S(1)}, u32[]{:S(2)}, u32[]{:S(2)}) collective-permute-start(bf16[640,1024]{1,0:T(8,128)(2,1)} %get-tuple-element.24), channel_id=1, source_target_pairs={{0,2},{2,4},{4,6},{6,8},{8,10},{10,12},{12,14},{1,3},{3,5},{5,7},{... | collective-permute-start | bytes 3932168 | tf_op jit(solution)/shard_map/ppermute | solution.py:27
  19.9 20.5 %shard_map.114 = (bf16[768,4096]{1,0:T(8,128)(2,1)}, f32[4096,128]{1,0:T(8,128)}, bf16[4096,128]{1,0:T(8,128)(2,1)}, bf16[640,1024]{1,0:T(8,128)(2,1)}, bf16[640...) custom-call(s32[4]{0:T(128)} %get-tuple-element.16.refs_0_.meta, ...), custom_call_target="tpu_custom_call", output_to_operand_aliasing={{0}: (6, {}), {1}: (7, {}), {2}: (8, {})} | custom-call | flops 30000001024 | bytes 8000000 | tf_op jit(solution)/shard_map/pallas_call | solution.py:252
  40.4 0.0 copy-start.1
  40.4 15.7 %all-to-all-start = ((bf16[8,8,64,128]{3,2,1,0:T(8,128)(2,1)}), bf16[8,8,64,128]{3,2,1,0:T(8,128)(2,1)}, u32[]{:S(2)}, u32[]{:S(2)}) async-start(bf16[8,8,64,128]{3,2,1,0:T(8,128)(2,1)} %bitcast.6), calls=%async_computation | async-start | bytes 2097152 | tf_op jit(solution)/shard_map/all_to_all | solution.py:354
  56.1 3.4 %collective-permute-start = (bf16[640,1024]{1,0:T(8,128)(2,1)}, bf16[640,1024]{1,0:T(8,128)(2,1)S(1)}, u32[]{:S(2)}, u32[]{:S(2)}) collective-permute-start(bf16[640,1024]{1,0:T(8,128)(2,1)} %get-tuple-element.21), channel_id=1, source_target_pairs={{0,2},{2,4},{4,6},{6,8},{8,10},{10,12},{12,14},{1,3},{3,5},{5,7},{... | collective-permute-start | bytes 3932168 | tf_op jit(solution)/shard_map/ppermute | solution.py:27
  59.5 3.4 %collective-permute-start.1 = (bf16[640,1024]{1,0:T(8,128)(2,1)}, bf16[640,1024]{1,0:T(8,128)(2,1)}, u32[]{:S(2)}, u32[]{:S(2)}) collective-permute-start(bf16[640,1024]{1,0:T(8,128)(2,1)} %get-tuple-element.22), channel_id=1, source_target_pairs={{0,2},{2,4},{4,6},{6,8},{8,10},{10,12},{12,14},{1,3},{3,5},{5,7},{... | collective-permute-start | bytes 3932168 | tf_op jit(solution)/shard_map/ppermute | solution.py:27
  62.9 3.4 %collective-permute-start.2 = (bf16[640,1024]{1,0:T(8,128)(2,1)}, bf16[640,1024]{1,0:T(8,128)(2,1)}, u32[]{:S(2)}, u32[]{:S(2)}) collective-permute-start(bf16[640,1024]{1,0:T(8,128)(2,1)} %get-tuple-element.23), channel_id=1, source_target_pairs={{0,2},{2,4},{4,6},{6,8},{8,10},{10,12},{12,14},{1,3},{3,5},{5,7},{... | collective-permute-start | bytes 3932168 | tf_op jit(solution)/shard_map/ppermute | solution.py:27
  66.3 0.0 collective-permute-done.3.moved_ref
  66.3 0.0 copy-done.1
  66.3 0.6 shard_map.115.rest_0_
  66.9 11.7 %all-to-all-done.arrived_ref = bf16[8,8,64,128]{3,2,1,0:T(8,128)(2,1)} async-done(((bf16[8,8,64,128]{3,2,1,0:T(8,128)(2,1)}), bf16[8,8,64,128]{3,2,1,0:T(8,128)(2,1)}, u32[]{:S(2)}, u32[]{:S(2)}) %all-to-all-start) | async-done | bytes 1048608 | tf_op jit(solution)/shard_map/all_to_all | solution.py:354
  78.6 8.0 %shard_map.116.rest_1_ = f32[8,12,64,128]{3,2,1,0:T(8,128)} custom-call(s32[12]{0:T(128)} %get-tuple-element.26.source, bf16[8,8,64,128]{3,2,1,0:T(8,128)(2,1)} %all-to-all-done.arrived_ref), custom_call_target="tpu_custom_call" | custom-call | bytes 5000000 | tf_op jit(solution)/shard_map/pallas_call | solution.py:307
  86.6 78.2 %collective-permute-done.2.moved_ref = bf16[640,1024]{1,0:T(8,128)(2,1)} collective-permute-done((bf16[640,1024]{1,0:T(8,128)(2,1)}, bf16[640,1024]{1,0:T(8,128)(2,1)}, u32[]{:S(2)}, u32[]{:S(2)}) %collective-permute-start.2) | collective-permute-done | bytes 1310752 | tf_op jit(solution)/shard_map/ppermute | solution.py:27
  164.8 0.0 copy-start
  164.8 1.9 %copy-done = f32[8,12,64,128]{3,2,1,0:T(8,128)S(1)} copy-done((f32[8,12,64,128]{3,2,1,0:T(8,128)S(1)}, f32[8,12,64,128]{3,2,1,0:T(8,128)}, u32[]{:S(2)}) %copy-start) | copy-done | bytes 3145752
  166.7 1.9 %shard_map.117.rest_0_ = bf16[768,4096]{1,0:T(8,128)(2,1)} custom-call(s32[4]{0:T(128)S(1)} %copy-done.1, bf16[640,1024]{1,0:T(8,128)(2,1)} %collective-permute-done.2.moved_ref, bf16[768,4096]{1,0:T(8,128)(2,1)} %shard_map.115.rest_0_, f32[8,12,64,128]{3,2,1,0:T(8,128)S(1)} %copy-done), custom_call_target="tpu_custom_call", output_to_operand_aliasing={{}: (2, {})} | custom-call | flops 30000001024 | bytes 2000000 | tf_op jit(solution)/shard_map/pallas_call | solution.py:283
  168.6 0.0 collective-permute-done.1.moved_ref
  168.6 1.9 %shard_map.118.rest_0_ = bf16[768,4096]{1,0:T(8,128)(2,1)} custom-call(s32[4]{0:T(128)S(1)} %copy-done.1, bf16[640,1024]{1,0:T(8,128)(2,1)} %collective-permute-done.1.moved_ref, bf16[768,4096]{1,0:T(8,128)(2,1)} %shard_map.117.rest_0_), custom_call_target="tpu_custom_call", output_to_operand_aliasing={{}: (2, {})} | custom-call | flops 30000001024 | bytes 2000000 | tf_op jit(solution)/shard_map/pallas_call | solution.py:283
  170.5 0.0 collective-permute-done.moved_ref
  170.5 0.6 shard_map.119
Async XLA Ops:
  12.0 54.2 %collective-permute-start.3 = (bf16[640,1024]{1,0:T(8,128)(2,1)}, bf16[640,1024]{1,0:T(8,128)(2,1)S(1)}, u32[]{:S(2)}, u32[]{:S(2)}) collective-permute-start(bf16[640,1024]{1,0:T(8,128)(2,1)} %get-tuple-element.24), channel_id=1, source_target_pairs={{0,2},{2,4},{4,6},{6,8},{8,10},{10,12},{12,14},{1,3},{3,5},{5,7},{... | collective-permute-start | bytes 3932168 | tf_op jit(solution)/shard_map/ppermute | solution.py:27
  40.4 25.9 %copy-start.1 = (s32[4]{0:T(128)S(1)}, s32[4]{0:T(128)}, u32[]{:S(2)}) copy-start(s32[4]{0:T(128)} %get-tuple-element.16.refs_0_.meta) | copy-start | bytes 52
  40.4 38.2 %all-to-all-start = ((bf16[8,8,64,128]{3,2,1,0:T(8,128)(2,1)}), bf16[8,8,64,128]{3,2,1,0:T(8,128)(2,1)}, u32[]{:S(2)}, u32[]{:S(2)}) async-start(bf16[8,8,64,128]{3,2,1,0:T(8,128)(2,1)} %bitcast.6), calls=%async_computation | async-start | bytes 2097152 | tf_op jit(solution)/shard_map/all_to_all | solution.py:354
  56.1 114.4 %collective-permute-start = (bf16[640,1024]{1,0:T(8,128)(2,1)}, bf16[640,1024]{1,0:T(8,128)(2,1)S(1)}, u32[]{:S(2)}, u32[]{:S(2)}) collective-permute-start(bf16[640,1024]{1,0:T(8,128)(2,1)} %get-tuple-element.21), channel_id=1, source_target_pairs={{0,2},{2,4},{4,6},{6,8},{8,10},{10,12},{12,14},{1,3},{3,5},{5,7},{... | collective-permute-start | bytes 3932168 | tf_op jit(solution)/shard_map/ppermute | solution.py:27
  59.5 109.1 %collective-permute-start.1 = (bf16[640,1024]{1,0:T(8,128)(2,1)}, bf16[640,1024]{1,0:T(8,128)(2,1)}, u32[]{:S(2)}, u32[]{:S(2)}) collective-permute-start(bf16[640,1024]{1,0:T(8,128)(2,1)} %get-tuple-element.22), channel_id=1, source_target_pairs={{0,2},{2,4},{4,6},{6,8},{8,10},{10,12},{12,14},{1,3},{3,5},{5,7},{... | collective-permute-start | bytes 3932168 | tf_op jit(solution)/shard_map/ppermute | solution.py:27
  62.9 101.9 %collective-permute-start.2 = (bf16[640,1024]{1,0:T(8,128)(2,1)}, bf16[640,1024]{1,0:T(8,128)(2,1)}, u32[]{:S(2)}, u32[]{:S(2)}) collective-permute-start(bf16[640,1024]{1,0:T(8,128)(2,1)} %get-tuple-element.23), channel_id=1, source_target_pairs={{0,2},{2,4},{4,6},{6,8},{8,10},{10,12},{12,14},{1,3},{3,5},{5,7},{... | collective-permute-start | bytes 3932168 | tf_op jit(solution)/shard_map/ppermute | solution.py:27
  164.8 1.9 %copy-start = (f32[8,12,64,128]{3,2,1,0:T(8,128)S(1)}, f32[8,12,64,128]{3,2,1,0:T(8,128)}, u32[]{:S(2)}) copy-start(f32[8,12,64,128]{3,2,1,0:T(8,128)} %shard_map.116.rest_1_) | copy-start | bytes 9437188
